TPU v7x, 512 devices: a whole 4x8x8 slice. The times are simulated.
512 devices in a mesh: lat: 16 (over x_lo, z), lon: 32 (over x_hi, y, core).
Axes of the slice: x: 4 (x_hi: 2, x_lo: 2; x = x_hi * 2 + x_lo), y: 8, z: 8, core: 2. Of those that a mesh axis runs over, the one named last changes fastest.
Arguments:
- fields: bfloat16 [75, 128, 4096], P(None, 'lat', 'lon'), may hold values from -6 to 6
- mask: int32 [128, 4096], P('lat', 'lon'), may hold values from 0 to 1, as said below
- w1: bfloat16 [9, 48, 75], replicated, may hold values from -0.25 to 0.25
- w2: bfloat16 [9, 48, 48], replicated, may hold values from -0.3125 to 0.3125
- cotangent: bfloat16 [48, 128, 4096], P(None, 'lat', 'lon'), may hold values from -6 to 6
Outputs:
- output: bfloat16 [48, 128, 4096], P(None, 'lat', 'lon')
- dx: bfloat16 [75, 128, 4096], P(None, 'lat', 'lon')
- dw1: float32 [9, 48, 75], replicated
- dw2: float32 [9, 48, 48], replicated
Inputs may be any that keep to these rules, and one draw needn't show every extreme that they name: `mask`: rows below 8 are sea. Each aligned block of 8 x 8 grid points is all land or all sea.
All inputs are finite; a program needn't handle non-finite values.
Results may differ from a plain program's by a relative error of at most 0.017.
Values may be sent and summed in bfloat16 or wider, within the bound.
A program may use at most 64 MiB of HBM per device.

v0:
```python
import math
import jax
import jax.numpy as jnp
from jax import lax
from jax.sharding import PartitionSpec as P


def from_partner(x, axis, bit):
    return lax.ppermute(x, axis, [(i, i ^ 1 << bit) for i in range(lax.axis_size(axis))])


def extended(x, sides, width, wrap):
    for axis, dim in sides:
        peers, length = (lax.axis_size(axis), x.shape[dim])
        up = [(i, (i + 1) % peers) for i in range(peers if wrap else peers - 1)]
        down = [(j, i) for i, j in up]
        last = lax.slice_in_dim(x, length - width, length, axis=dim)
        leading = lax.slice_in_dim(x, 0, width, axis=dim)
        before = lax.ppermute(last, axis, up)
        after = lax.ppermute(leading, axis, down)
        x = jnp.concatenate([before, x, after], axis=dim)
    return x


def gelu_parts(a):
    coeff = 0.7978845608
    inner = coeff * (a + 0.044715 * a * a * a)
    tval = jnp.tanh(inner)
    value = 0.5 * a * (1.0 + tval)
    slope = 0.5 * (1.0 + tval) + 0.5 * a * (1.0 - tval * tval) * coeff * (1.0 + 0.134145 * a * a)
    return (value, slope)


def at_top():
    return lax.axis_index("lat") == lax.axis_size("lat") - 1


def bit_order():
    count = lax.axis_size("lon").bit_length() - 1
    return list(range(count))


def mirror_fwd(row_top):
    moved = row_top
    for bitnum in bit_order():
        moved = from_partner(moved, "lon", bitnum)
    return moved[:, ::-1]


def mirror_back(row_top):
    moved = row_top
    for bitnum in bit_order():
        moved = from_partner(moved.astype(jnp.bfloat16), "lon", bitnum).astype(moved.dtype)
    return moved[:, ::-1]


def extend(field):
    rows_ext = extended(field, (("lat", 1),), 1, False)
    folded = mirror_fwd(field[:, -1, :])
    top_row = jnp.where(at_top(), folded, rows_ext[:, -1, :])
    rows_ext = jnp.concatenate([rows_ext[:, :-1, :], top_row[:, None, :]], axis=1)
    return extended(rows_ext, (("lon", 2),), 1, True)


def retract(padded):
    edges = jnp.stack((padded[:, :, 0], padded[:, :, -1]), 0)
    edge_got = extended(edges, (("lon", 0),), 1, True)
    inner = padded[:, :, 1:-1]
    inner = inner.at[:, :, 0].add(edge_got[0]).at[:, :, -1].add(edge_got[3])
    rims = jnp.stack((inner[:, 0, :], inner[:, -1, :]), 0)
    rim_got = extended(rims.astype(jnp.bfloat16), (("lat", 0),), 1, False).astype(rims.dtype)
    folded = mirror_back(inner[:, -1, :])
    result = inner[:, 1:-1, :]
    top_add = rim_got[3] + jnp.where(at_top(), folded, 0.0)
    return result.at[:, 0, :].add(rim_got[0]).at[:, -1, :].add(top_add)


def conv(padded, kernel):
    rows_n = padded.shape[1] - 2
    cols_n = padded.shape[2] - 2
    total = jnp.zeros((kernel.shape[1], rows_n, cols_n), jnp.float32)
    for tap in range(9):
        drow, dcol = (tap // 3, tap % 3)
        total = total + jnp.einsum(
            "oi,ihw->ohw",
            kernel[tap],
            padded[:, drow : drow + rows_n, dcol : dcol + cols_n],
            preferred_element_type=jnp.float32,
        )
    return total


def tconv(grad, kernel):
    rows_n = grad.shape[1]
    cols_n = grad.shape[2]
    wide = jnp.pad(grad, ((0, 0), (2, 2), (2, 2)))
    total = jnp.zeros((kernel.shape[2], rows_n + 2, cols_n + 2), jnp.float32)
    for tap in range(9):
        drow, dcol = (tap // 3, tap % 3)
        total = total + jnp.einsum(
            "oi,ohw->ihw",
            kernel[tap],
            wide[:, 2 - drow : 4 - drow + rows_n, 2 - dcol : 4 - dcol + cols_n],
            preferred_element_type=jnp.float32,
        )
    return total


def wgrad(grad, padded):
    rows_n = grad.shape[1]
    cols_n = grad.shape[2]
    terms = []
    for tap in range(9):
        drow, dcol = (tap // 3, tap % 3)
        terms.append(
            jnp.einsum(
                "ohw,ihw->oi",
                grad,
                padded[:, drow : drow + rows_n, dcol : dcol + cols_n],
                preferred_element_type=jnp.float32,
            )
        )
    return jnp.stack(terms, 0)


def body(fields, mask, w1, w2, cotangent):
    sea = mask.astype(jnp.float32)
    x_ext = extend(fields)
    value, slope = gelu_parts(conv(x_ext, w1))
    hidden = (value * sea).astype(jnp.bfloat16)
    gate = slope * sea
    h_ext = extend(hidden)
    out_block = (conv(h_ext, w2) * sea).astype(jnp.bfloat16)
    grad_out = cotangent * mask.astype(jnp.bfloat16)
    term_w2 = wgrad(grad_out, h_ext)
    grad_h_ext = tconv(grad_out, w2)
    grad_h = retract(grad_h_ext)
    grad_a = (grad_h * gate).astype(jnp.bfloat16)
    term_w1 = wgrad(grad_a, x_ext)
    grad_x_ext = tconv(grad_a, w1)
    dx = retract(grad_x_ext).astype(jnp.bfloat16)
    grad_w1, grad_w2 = lax.psum((term_w1, term_w2), ("lat", "lon"))
    cells = fields.shape[1] * fields.shape[2] * lax.axis_size("lat") * lax.axis_size("lon")
    factor = 1.0 / math.sqrt(cells)
    return (out_block, dx, grad_w1 * factor, grad_w2 * factor)


def solution(mesh):
    in_specs = (P(None, "lat", "lon"), P("lat", "lon"), P(), P(), P(None, "lat", "lon"))
    out_specs = (P(None, "lat", "lon"), P(None, "lat", "lon"), P(), P())
    return jax.shard_map(body, mesh=mesh, in_specs=in_specs, out_specs=out_specs, check_vma=False)
```

profile of v0, /device:TPU:1, one launch (start us, length us, event | category | flops | bytes accessed | tf_op | source)
XLA Modules:
  0.0 454.7 jit_solution(2405748562817227738)
XLA Ops:
  8.0 0.9 copy_multiply_fusion
  11.8 4.6 %collective-permute-start.18 = (f32[1,48,10]{1,0,2:T(1,128)S(1)}, f32[1,48,10]{1,0,2:T(1,128)S(1)}, u32[]{:S(2)}, u32[]{:S(2)}) collective-permute-start(f32[1,48,10]{1,0,2:T(1,128)S(1)} %stack_squeeze.28), channel_id=1, source_target_pairs={{0,1},{1,2},{2,3},{3,4},{4,5},{5,6},{6,7},{7,8},{8,9},{9,10},{10,1... | collective-permute-start | bytes 5768 | tf_op jit(solution)/shard_map/ppermute | solution.py:19
  16.4 6.1 %collective-permute-start.19 = (f32[1,48,10]{1,0,2:T(1,128)S(1)}, f32[1,48,10]{1,0,2:T(1,128)S(1)}, u32[]{:S(2)}, u32[]{:S(2)}) collective-permute-start(f32[1,48,10]{1,0,2:T(1,128)S(1)} %stack_squeeze.29), channel_id=1, source_target_pairs={{1,0},{2,1},{3,2},{4,3},{5,4},{6,5},{7,6},{8,7},{9,8},{10,9},{11,1... | collective-permute-start | bytes 5768 | tf_op jit(solution)/shard_map/ppermute | solution.py:20
  22.7 7.3 %collective-permute-start.1 = (bf16[75,128]{0,1:T(8,128)(2,1)S(1)}, bf16[75,128]{0,1:T(8,128)(2,1)S(1)}, u32[]{:S(2)}, u32[]{:S(2)}) collective-permute-start(bf16[75,128]{0,1:T(8,128)(2,1)S(1)} %bitcast.327), channel_id=1, source_target_pairs={{0,1},{1,0},{2,3},{3,2},{4,5},{5,4},{6,7},{7,6},{8,9},{9,8},{10,11... | collective-permute-start | bytes 57608 | tf_op jit(solution)/shard_map/ppermute | solution.py:9
  30.9 1.0 scatter-add.29
  31.9 1.9 collective-permute-start.2
  33.8 1.9 collective-permute-start.22
  35.8 1.1 collective-permute-done.22
  36.9 3.4 collective-permute-start.23
  40.3 1.9 collective-permute-start.3
  42.2 1.3 collective-permute-start.21
  43.5 4.3 collective-permute-start.24
  47.8 4.0 collective-permute-start.20
  51.8 1.9 collective-permute-start
  53.9 1.4 collective-permute-start.6
  55.4 2.8 collective-permute-start.25
  58.1 6.4 %collective-permute-start.4 = (bf16[75,128]{0,1:T(8,128)(2,1)S(1)}, bf16[75,128]{0,1:T(8,128)(2,1)S(1)}, u32[]{:S(2)}, u32[]{:S(2)}) collective-permute-start(bf16[75,128]{0,1:T(8,128)(2,1)S(1)} %collective-permute-done.3), channel_id=1, source_target_pairs={{0,8},{1,9},{2,10},{3,11},{4,12},{5,13},{6,14},{7,15},{8,0},{9,1},... | collective-permute-start | bytes 57608 | tf_op jit(solution)/shard_map/ppermute | solution.py:9
  64.7 2.0 collective-permute-start.26
  66.9 4.8 %collective-permute-start.5 = (bf16[75,128]{0,1:T(8,128)(2,1)S(1)}, bf16[75,128]{0,1:T(8,128)(2,1)S(1)}, u32[]{:S(2)}, u32[]{:S(2)}) collective-permute-start(bf16[75,128]{0,1:T(8,128)(2,1)S(1)} %collective-permute-done.4), channel_id=1, source_target_pairs={{0,16},{1,17},{2,18},{3,19},{4,20},{5,21},{6,22},{7,23},{8,24},{9,... | collective-permute-start | bytes 57608 | tf_op jit(solution)/shard_map/ppermute | solution.py:9
  72.0 1.1 collective-permute-done.5
  73.4 6.0 %collective-permute-start.8 = (bf16[75,10,1]{2,0,1:T(8,128)(2,1)S(1)}, bf16[75,10,1]{2,0,1:T(8,128)(2,1)S(1)}, u32[]{:S(2)}, u32[]{:S(2)}) collective-permute-start(bf16[75,10,1]{2,0,1:T(8,128)(2,1)S(1)} %get-tuple-element.134), channel_id=1, source_target_pairs={{1,0},{2,1},{3,2},{4,3},{5,4},{6,5},{7,6},{8,7},{9,8},{10,9},{11,1... | collective-permute-start | bytes 4508 | tf_op jit(solution)/shard_map/ppermute | solution.py:20
  79.5 3.1 collective-permute-start.7
  82.6 1.5 collective-permute-done.8
  84.1 1.2 collective-permute-done.7
  88.0 4.5 collective-permute-start.9
  92.5 7.7 %collective-permute-start.10 = (bf16[48,128]{1,0:T(8,128)(2,1)S(1)}, bf16[48,128]{1,0:T(8,128)(2,1)S(1)}, u32[]{:S(2)}, u32[]{:S(2)}) collective-permute-start(bf16[48,128]{1,0:T(8,128)(2,1)S(1)} %get-tuple-element.145), channel_id=1, source_target_pairs={{0,1},{1,0},{2,3},{3,2},{4,5},{5,4},{6,7},{7,6},{8,9},{9,8},{10,11... | collective-permute-start | bytes 36872 | tf_op jit(solution)/shard_map/ppermute | solution.py:9
  100.2 1.3 collective-permute-start.15
  106.6 1.9 collective-permute-start.27
  108.8 2.4 collective-permute-start.28
  111.3 2.7 collective-permute-done.28
  114.1 1.9 collective-permute-start.11
  116.1 5.3 %collective-permute-start.31 = (bf16[75,128]{0,1:T(8,128)(2,1)S(1)}, bf16[75,128]{0,1:T(8,128)(2,1)S(1)}, u32[]{:S(2)}, u32[]{:S(2)}) collective-permute-start(bf16[75,128]{0,1:T(8,128)(2,1)S(1)} %get-tuple-element.126), channel_id=1, source_target_pairs={{0,1},{1,0},{2,3},{3,2},{4,5},{5,4},{6,7},{7,6},{8,9},{9,8},{10,11... | collective-permute-start | bytes 57608 | tf_op jit(solution)/shard_map/ppermute | solution.py:9
  121.4 1.9 collective-permute-start.12
  124.2 1.3 collective-permute-start.30
  125.5 6.1 %collective-permute-start.29 = (bf16[1,75,128]{1,2,0:T(8,128)(2,1)S(1)}, bf16[1,75,128]{1,2,0:T(8,128)(2,1)S(1)}, u32[]{:S(2)}, u32[]{:S(2)}) collective-permute-start(bf16[1,75,128]{1,2,0:T(8,128)(2,1)S(1)} %get-tuple-element.128), channel_id=1, source_target_pairs={{0,32},{32,64},{64,96},{96,128},{128,160},{160,192},{192,224},{224... | collective-permute-start | bytes 57608 | tf_op jit(solution)/shard_map/ppermute | solution.py:19
  131.6 3.6 collective-permute-start.32
  135.3 8.4 %collective-permute-start.13 = (bf16[48,128]{1,0:T(8,128)(2,1)S(1)}, bf16[48,128]{1,0:T(8,128)(2,1)S(1)}, u32[]{:S(2)}, u32[]{:S(2)}) collective-permute-start(bf16[48,128]{1,0:T(8,128)(2,1)S(1)} %collective-permute-done.12), channel_id=1, source_target_pairs={{0,8},{1,9},{2,10},{3,11},{4,12},{5,13},{6,14},{7,15},{8,0},{9,1},... | collective-permute-start | bytes 36872 | tf_op jit(solution)/shard_map/ppermute | solution.py:9
  143.9 1.9 collective-permute-start.33
  145.8 2.7 collective-permute-start.14
  148.5 0.9 collective-permute-done.33
  149.4 5.3 %collective-permute-start.34 = (bf16[75,128]{0,1:T(8,128)(2,1)S(1)}, bf16[75,128]{0,1:T(8,128)(2,1)S(1)}, u32[]{:S(2)}, u32[]{:S(2)}) collective-permute-start(bf16[75,128]{0,1:T(8,128)(2,1)S(1)} %collective-permute-done.33), channel_id=1, source_target_pairs={{0,8},{1,9},{2,10},{3,11},{4,12},{5,13},{6,14},{7,15},{8,0},{9,1},... | collective-permute-start | bytes 57608 | tf_op jit(solution)/shard_map/ppermute | solution.py:9
  155.0 4.4 collective-permute-start.17
  159.4 3.3 collective-permute-start.16
  163.3 1.2 collective-permute-done.16
  167.4 4.1 collective-permute-start.35
  172.5 1.0 collective-permute-done.35
  174.5 271.0 %all-reduce.5.cloned.1.call-done = (f32[9,48,75]{2,1,0:T(8,128)}, f32[9,48,48]{2,1,0:T(8,128)}) async-done(((f32[9,48,75]{2,1,0:T(8,128)}, f32[9,48,48]{2,1,0:T(8,128)}), (f32[9,48,75]{2,1,0:T(8,128)}, f32[9,48,48]{2,1,0:T(8,128)})) %all-reduce.5.cloned.1.call-update) | async-done | bytes 212560 | tf_op jit(solution)/shard_map/psum | solution.py:142
  445.5 1.7 broadcast_multiply_fusion.1
  (143 shorter events, 20.9 us)
Async XLA Ops:
  7.2 1.7 copy-start.1
  7.2 438.3 %all-reduce.5.cloned.1.call-start = ((), (), s32[]{:S(2)}) async-start(), calls=%async_computation | async-start | bytes 884736 | tf_op jit(solution)/shard_map/psum | solution.py:142
  11.5 11.0 %copy-start = (bf16[75,8,128]{2,1,0:T(8,128)(2,1)S(1)}, bf16[75,8,128]{2,1,0:T(8,128)(2,1)}, u32[]{:S(2)}) copy-start(bf16[75,8,128]{2,1,0:T(8,128)(2,1)} %param.21) | copy-start | bytes 460804
  11.8 18.5 %collective-permute-start.18 = (f32[1,48,10]{1,0,2:T(1,128)S(1)}, f32[1,48,10]{1,0,2:T(1,128)S(1)}, u32[]{:S(2)}, u32[]{:S(2)}) collective-permute-start(f32[1,48,10]{1,0,2:T(1,128)S(1)} %stack_squeeze.28), channel_id=1, source_target_pairs={{0,1},{1,2},{2,3},{3,4},{4,5},{5,6},{6,7},{7,8},{8,9},{9,10},{10,1... | collective-permute-start | bytes 5768 | tf_op jit(solution)/shard_map/ppermute | solution.py:19
  16.4 13.7 %collective-permute-start.19 = (f32[1,48,10]{1,0,2:T(1,128)S(1)}, f32[1,48,10]{1,0,2:T(1,128)S(1)}, u32[]{:S(2)}, u32[]{:S(2)}) collective-permute-start(f32[1,48,10]{1,0,2:T(1,128)S(1)} %stack_squeeze.29), channel_id=1, source_target_pairs={{1,0},{2,1},{3,2},{4,3},{5,4},{6,5},{7,6},{8,7},{9,8},{10,9},{11,1... | collective-permute-start | bytes 5768 | tf_op jit(solution)/shard_map/ppermute | solution.py:20
  22.7 9.2 %collective-permute-start.1 = (bf16[75,128]{0,1:T(8,128)(2,1)S(1)}, bf16[75,128]{0,1:T(8,128)(2,1)S(1)}, u32[]{:S(2)}, u32[]{:S(2)}) collective-permute-start(bf16[75,128]{0,1:T(8,128)(2,1)S(1)} %bitcast.327), channel_id=1, source_target_pairs={{0,1},{1,0},{2,3},{3,2},{4,5},{5,4},{6,7},{7,6},{8,9},{9,8},{10,11... | collective-permute-start | bytes 57608 | tf_op jit(solution)/shard_map/ppermute | solution.py:9
  31.9 8.4 %collective-permute-start.2 = (bf16[75,128]{0,1:T(8,128)(2,1)S(1)}, bf16[75,128]{0,1:T(8,128)(2,1)S(1)}, u32[]{:S(2)}, u32[]{:S(2)}) collective-permute-start(bf16[75,128]{0,1:T(8,128)(2,1)S(1)} %collective-permute-done.1), channel_id=1, source_target_pairs={{0,2},{1,3},{2,0},{3,1},{4,6},{5,7},{6,4},{7,5},{8,10},{9,11},{10,... | collective-permute-start | bytes 57608 | tf_op jit(solution)/shard_map/ppermute | solution.py:9
  33.8 3.1 collective-permute-start.22
  36.9 6.6 %collective-permute-start.23 = (bf16[48,128]{1,0:T(8,128)(2,1)S(1)}, bf16[48,128]{1,0:T(8,128)(2,1)S(1)}, u32[]{:S(2)}, u32[]{:S(2)}) collective-permute-start(bf16[48,128]{1,0:T(8,128)(2,1)S(1)} %collective-permute-done.22), channel_id=1, source_target_pairs={{0,2},{1,3},{2,0},{3,1},{4,6},{5,7},{6,4},{7,5},{8,10},{9,11},{10,... | collective-permute-start | bytes 36872 | tf_op jit(solution)/shard_map/ppermute | solution.py:9
  40.3 17.9 %collective-permute-start.3 = (bf16[75,128]{0,1:T(8,128)(2,1)S(1)}, bf16[75,128]{0,1:T(8,128)(2,1)S(1)}, u32[]{:S(2)}, u32[]{:S(2)}) collective-permute-start(bf16[75,128]{0,1:T(8,128)(2,1)S(1)} %collective-permute-done.2), channel_id=1, source_target_pairs={{0,4},{1,5},{2,6},{3,7},{4,0},{5,1},{6,2},{7,3},{8,12},{9,13},{10,... | collective-permute-start | bytes 57608 | tf_op jit(solution)/shard_map/ppermute | solution.py:9
  42.2 11.7 %collective-permute-start.21 = (bf16[1,48,128]{2,1,0:T(8,128)(2,1)S(1)}, bf16[1,48,128]{2,1,0:T(8,128)(2,1)S(1)}, u32[]{:S(2)}, u32[]{:S(2)}) collective-permute-start(bf16[1,48,128]{2,1,0:T(8,128)(2,1)S(1)} %get-tuple-element.130), channel_id=1, source_target_pairs={{32,0},{64,32},{96,64},{128,96},{160,128},{192,160},{224,192},{256... | collective-permute-start | bytes 36872 | tf_op jit(solution)/shard_map/ppermute | solution.py:20
  43.5 11.8 %collective-permute-start.24 = (bf16[48,128]{1,0:T(8,128)(2,1)S(1)}, bf16[48,128]{1,0:T(8,128)(2,1)S(1)}, u32[]{:S(2)}, u32[]{:S(2)}) collective-permute-start(bf16[48,128]{1,0:T(8,128)(2,1)S(1)} %collective-permute-done.23), channel_id=1, source_target_pairs={{0,4},{1,5},{2,6},{3,7},{4,0},{5,1},{6,2},{7,3},{8,12},{9,13},{10,... | collective-permute-start | bytes 36872 | tf_op jit(solution)/shard_map/ppermute | solution.py:9
  47.8 16.8 %collective-permute-start.20 = (bf16[1,48,128]{2,1,0:T(8,128)(2,1)S(1)}, bf16[1,48,128]{2,1,0:T(8,128)(2,1)S(1)}, u32[]{:S(2)}, u32[]{:S(2)}) collective-permute-start(bf16[1,48,128]{2,1,0:T(8,128)(2,1)S(1)} %get-tuple-element.131), channel_id=1, source_target_pairs={{0,32},{32,64},{64,96},{96,128},{128,160},{160,192},{192,224},{224... | collective-permute-start | bytes 36872 | tf_op jit(solution)/shard_map/ppermute | solution.py:19
  51.8 12.8 %collective-permute-start = (bf16[75,1,128]{0,2,1:T(8,128)(2,1)S(1)}, bf16[75,1,128]{0,2,1:T(8,128)(2,1)S(1)}, u32[]{:S(2)}, u32[]{:S(2)}) collective-permute-start(bf16[75,1,128]{0,2,1:T(8,128)(2,1)S(1)} %copy.200), channel_id=1, source_target_pairs={{0,32},{32,64},{64,96},{96,128},{128,160},{160,192},{192,224},{224... | collective-permute-start | bytes 57608 | tf_op jit(solution)/shard_map/ppermute | solution.py:19
  53.9 17.8 %copy-start.2 = (bf16[9,48,75]{2,1,0:T(8,128)(2,1)S(1)}, bf16[9,48,75]{2,1,0:T(8,128)(2,1)}, u32[]{:S(2)}) copy-start(bf16[9,48,75]{2,1,0:T(8,128)(2,1)} %param.23) | copy-start | bytes 194404
  53.9 19.2 %collective-permute-start.6 = (bf16[75,1,128]{0,2,1:T(8,128)(2,1)S(1)}, bf16[75,1,128]{0,2,1:T(8,128)(2,1)S(1)}, u32[]{:S(2)}, u32[]{:S(2)}) collective-permute-start(bf16[75,1,128]{0,2,1:T(8,128)(2,1)S(1)} %copy.201), channel_id=1, source_target_pairs={{32,0},{64,32},{96,64},{128,96},{160,128},{192,160},{224,192},{256... | collective-permute-start | bytes 57608 | tf_op jit(solution)/shard_map/ppermute | solution.py:20
  55.4 9.4 %collective-permute-start.25 = (bf16[48,128]{1,0:T(8,128)(2,1)S(1)}, bf16[48,128]{1,0:T(8,128)(2,1)S(1)}, u32[]{:S(2)}, u32[]{:S(2)}) collective-permute-start(bf16[48,128]{1,0:T(8,128)(2,1)S(1)} %collective-permute-done.24), channel_id=1, source_target_pairs={{0,8},{1,9},{2,10},{3,11},{4,12},{5,13},{6,14},{7,15},{8,0},{9,1},... | collective-permute-start | bytes 36872 | tf_op jit(solution)/shard_map/ppermute | solution.py:9
  58.1 8.8 %collective-permute-start.4 = (bf16[75,128]{0,1:T(8,128)(2,1)S(1)}, bf16[75,128]{0,1:T(8,128)(2,1)S(1)}, u32[]{:S(2)}, u32[]{:S(2)}) collective-permute-start(bf16[75,128]{0,1:T(8,128)(2,1)S(1)} %collective-permute-done.3), channel_id=1, source_target_pairs={{0,8},{1,9},{2,10},{3,11},{4,12},{5,13},{6,14},{7,15},{8,0},{9,1},... | collective-permute-start | bytes 57608 | tf_op jit(solution)/shard_map/ppermute | solution.py:9
  64.7 7.2 %collective-permute-start.26 = (bf16[48,128]{1,0:T(8,128)(2,1)S(1)}, bf16[48,128]{1,0:T(8,128)(2,1)S(1)}, u32[]{:S(2)}, u32[]{:S(2)}) collective-permute-start(bf16[48,128]{1,0:T(8,128)(2,1)S(1)} %collective-permute-done.25), channel_id=1, source_target_pairs={{0,16},{1,17},{2,18},{3,19},{4,20},{5,21},{6,22},{7,23},{8,24},{9,... | collective-permute-start | bytes 36872 | tf_op jit(solution)/shard_map/ppermute | solution.py:9
  66.9 6.2 %collective-permute-start.5 = (bf16[75,128]{0,1:T(8,128)(2,1)S(1)}, bf16[75,128]{0,1:T(8,128)(2,1)S(1)}, u32[]{:S(2)}, u32[]{:S(2)}) collective-permute-start(bf16[75,128]{0,1:T(8,128)(2,1)S(1)} %collective-permute-done.4), channel_id=1, source_target_pairs={{0,16},{1,17},{2,18},{3,19},{4,20},{5,21},{6,22},{7,23},{8,24},{9,... | collective-permute-start | bytes 57608 | tf_op jit(solution)/shard_map/ppermute | solution.py:9
  73.4 10.7 %collective-permute-start.8 = (bf16[75,10,1]{2,0,1:T(8,128)(2,1)S(1)}, bf16[75,10,1]{2,0,1:T(8,128)(2,1)S(1)}, u32[]{:S(2)}, u32[]{:S(2)}) collective-permute-start(bf16[75,10,1]{2,0,1:T(8,128)(2,1)S(1)} %get-tuple-element.134), channel_id=1, source_target_pairs={{1,0},{2,1},{3,2},{4,3},{5,4},{6,5},{7,6},{8,7},{9,8},{10,9},{11,1... | collective-permute-start | bytes 4508 | tf_op jit(solution)/shard_map/ppermute | solution.py:20
  79.5 5.8 %collective-permute-start.7 = (bf16[75,10,1]{2,0,1:T(8,128)(2,1)S(1)}, bf16[75,10,1]{2,0,1:T(8,128)(2,1)S(1)}, u32[]{:S(2)}, u32[]{:S(2)}) collective-permute-start(bf16[75,10,1]{2,0,1:T(8,128)(2,1)S(1)} %get-tuple-element.135), channel_id=1, source_target_pairs={{0,1},{1,2},{2,3},{3,4},{4,5},{5,6},{6,7},{7,8},{8,9},{9,10},{10,1... | collective-permute-start | bytes 4508 | tf_op jit(solution)/shard_map/ppermute | solution.py:19
  88.0 37.5 %collective-permute-start.9 = (bf16[48,1,128]{2,0,1:T(8,128)(2,1)S(1)}, bf16[48,1,128]{2,0,1:T(8,128)(2,1)S(1)}, u32[]{:S(2)}, u32[]{:S(2)}) collective-permute-start(bf16[48,1,128]{2,0,1:T(8,128)(2,1)S(1)} %get-tuple-element.144), channel_id=1, source_target_pairs={{0,32},{32,64},{64,96},{96,128},{128,160},{160,192},{192,224},{224... | collective-permute-start | bytes 36872 | tf_op jit(solution)/shard_map/ppermute | solution.py:19
  92.5 21.6 %collective-permute-start.10 = (bf16[48,128]{1,0:T(8,128)(2,1)S(1)}, bf16[48,128]{1,0:T(8,128)(2,1)S(1)}, u32[]{:S(2)}, u32[]{:S(2)}) collective-permute-start(bf16[48,128]{1,0:T(8,128)(2,1)S(1)} %get-tuple-element.145), channel_id=1, source_target_pairs={{0,1},{1,0},{2,3},{3,2},{4,5},{5,4},{6,7},{7,6},{8,9},{9,8},{10,11... | collective-permute-start | bytes 36872 | tf_op jit(solution)/shard_map/ppermute | solution.py:9
  100.2 54.6 %collective-permute-start.15 = (bf16[48,1,128]{2,0,1:T(8,128)(2,1)S(1)}, bf16[48,1,128]{2,0,1:T(8,128)(2,1)S(1)}, u32[]{:S(2)}, u32[]{:S(2)}) collective-permute-start(bf16[48,1,128]{2,0,1:T(8,128)(2,1)S(1)} %get-tuple-element.146), channel_id=1, source_target_pairs={{32,0},{64,32},{96,64},{128,96},{160,128},{192,160},{224,192},{256... | collective-permute-start | bytes 36872 | tf_op jit(solution)/shard_map/ppermute | solution.py:20
  106.6 4.6 %collective-permute-start.27 = (f32[1,75,10]{1,0,2:T(1,128)S(1)}, f32[1,75,10]{1,0,2:T(1,128)S(1)}, u32[]{:S(2)}, u32[]{:S(2)}) collective-permute-start(f32[1,75,10]{1,0,2:T(1,128)S(1)} %get-tuple-element.125), channel_id=1, source_target_pairs={{0,1},{1,2},{2,3},{3,4},{4,5},{5,6},{6,7},{7,8},{8,9},{9,10},{10,1... | collective-permute-start | bytes 9008 | tf_op jit(solution)/shard_map/ppermute | solution.py:19
  108.8 5.2 %collective-permute-start.28 = (f32[1,75,10]{1,0,2:T(1,128)S(1)}, f32[1,75,10]{1,0,2:T(1,128)S(1)}, u32[]{:S(2)}, u32[]{:S(2)}) collective-permute-start(f32[1,75,10]{1,0,2:T(1,128)S(1)} %get-tuple-element.124), channel_id=1, source_target_pairs={{1,0},{2,1},{3,2},{4,3},{5,4},{6,5},{7,6},{8,7},{9,8},{10,9},{11,1... | collective-permute-start | bytes 9008 | tf_op jit(solution)/shard_map/ppermute | solution.py:20
  114.1 7.2 %collective-permute-start.11 = (bf16[48,128]{1,0:T(8,128)(2,1)S(1)}, bf16[48,128]{1,0:T(8,128)(2,1)S(1)}, u32[]{:S(2)}, u32[]{:S(2)}) collective-permute-start(bf16[48,128]{1,0:T(8,128)(2,1)S(1)} %collective-permute-done.10), channel_id=1, source_target_pairs={{0,2},{1,3},{2,0},{3,1},{4,6},{5,7},{6,4},{7,5},{8,10},{9,11},{10,... | collective-permute-start | bytes 36872 | tf_op jit(solution)/shard_map/ppermute | solution.py:9
  116.1 15.5 %collective-permute-start.31 = (bf16[75,128]{0,1:T(8,128)(2,1)S(1)}, bf16[75,128]{0,1:T(8,128)(2,1)S(1)}, u32[]{:S(2)}, u32[]{:S(2)}) collective-permute-start(bf16[75,128]{0,1:T(8,128)(2,1)S(1)} %get-tuple-element.126), channel_id=1, source_target_pairs={{0,1},{1,0},{2,3},{3,2},{4,5},{5,4},{6,7},{7,6},{8,9},{9,8},{10,11... | collective-permute-start | bytes 57608 | tf_op jit(solution)/shard_map/ppermute | solution.py:9
  121.4 13.9 %collective-permute-start.12 = (bf16[48,128]{1,0:T(8,128)(2,1)S(1)}, bf16[48,128]{1,0:T(8,128)(2,1)S(1)}, u32[]{:S(2)}, u32[]{:S(2)}) collective-permute-start(bf16[48,128]{1,0:T(8,128)(2,1)S(1)} %collective-permute-done.11), channel_id=1, source_target_pairs={{0,4},{1,5},{2,6},{3,7},{4,0},{5,1},{6,2},{7,3},{8,12},{9,13},{10,... | collective-permute-start | bytes 36872 | tf_op jit(solution)/shard_map/ppermute | solution.py:9
  123.5 0.7 copy-start.3
  124.2 24.2 %collective-permute-start.30 = (bf16[1,75,128]{1,2,0:T(8,128)(2,1)S(1)}, bf16[1,75,128]{1,2,0:T(8,128)(2,1)S(1)}, u32[]{:S(2)}, u32[]{:S(2)}) collective-permute-start(bf16[1,75,128]{1,2,0:T(8,128)(2,1)S(1)} %get-tuple-element.127), channel_id=1, source_target_pairs={{32,0},{64,32},{96,64},{128,96},{160,128},{192,160},{224,192},{256... | collective-permute-start | bytes 57608 | tf_op jit(solution)/shard_map/ppermute | solution.py:20
  125.5 22.9 %collective-permute-start.29 = (bf16[1,75,128]{1,2,0:T(8,128)(2,1)S(1)}, bf16[1,75,128]{1,2,0:T(8,128)(2,1)S(1)}, u32[]{:S(2)}, u32[]{:S(2)}) collective-permute-start(bf16[1,75,128]{1,2,0:T(8,128)(2,1)S(1)} %get-tuple-element.128), channel_id=1, source_target_pairs={{0,32},{32,64},{64,96},{96,128},{128,160},{160,192},{192,224},{224... | collective-permute-start | bytes 57608 | tf_op jit(solution)/shard_map/ppermute | solution.py:19
  131.6 12.3 %collective-permute-start.32 = (bf16[75,128]{0,1:T(8,128)(2,1)S(1)}, bf16[75,128]{0,1:T(8,128)(2,1)S(1)}, u32[]{:S(2)}, u32[]{:S(2)}) collective-permute-start(bf16[75,128]{0,1:T(8,128)(2,1)S(1)} %collective-permute-done.31), channel_id=1, source_target_pairs={{0,2},{1,3},{2,0},{3,1},{4,6},{5,7},{6,4},{7,5},{8,10},{9,11},{10,... | collective-permute-start | bytes 57608 | tf_op jit(solution)/shard_map/ppermute | solution.py:9
  135.3 10.5 %collective-permute-start.13 = (bf16[48,128]{1,0:T(8,128)(2,1)S(1)}, bf16[48,128]{1,0:T(8,128)(2,1)S(1)}, u32[]{:S(2)}, u32[]{:S(2)}) collective-permute-start(bf16[48,128]{1,0:T(8,128)(2,1)S(1)} %collective-permute-done.12), channel_id=1, source_target_pairs={{0,8},{1,9},{2,10},{3,11},{4,12},{5,13},{6,14},{7,15},{8,0},{9,1},... | collective-permute-start | bytes 36872 | tf_op jit(solution)/shard_map/ppermute | solution.py:9
  143.9 5.6 %collective-permute-start.33 = (bf16[75,128]{0,1:T(8,128)(2,1)S(1)}, bf16[75,128]{0,1:T(8,128)(2,1)S(1)}, u32[]{:S(2)}, u32[]{:S(2)}) collective-permute-start(bf16[75,128]{0,1:T(8,128)(2,1)S(1)} %collective-permute-done.32), channel_id=1, source_target_pairs={{0,4},{1,5},{2,6},{3,7},{4,0},{5,1},{6,2},{7,3},{8,12},{9,13},{10,... | collective-permute-start | bytes 57608 | tf_op jit(solution)/shard_map/ppermute | solution.py:9
  145.8 9.0 %collective-permute-start.14 = (bf16[48,128]{1,0:T(8,128)(2,1)S(1)}, bf16[48,128]{1,0:T(8,128)(2,1)S(1)}, u32[]{:S(2)}, u32[]{:S(2)}) collective-permute-start(bf16[48,128]{1,0:T(8,128)(2,1)S(1)} %collective-permute-done.13), channel_id=1, source_target_pairs={{0,16},{1,17},{2,18},{3,19},{4,20},{5,21},{6,22},{7,23},{8,24},{9,... | collective-permute-start | bytes 36872 | tf_op jit(solution)/shard_map/ppermute | solution.py:9
  149.4 17.9 %collective-permute-start.34 = (bf16[75,128]{0,1:T(8,128)(2,1)S(1)}, bf16[75,128]{0,1:T(8,128)(2,1)S(1)}, u32[]{:S(2)}, u32[]{:S(2)}) collective-permute-start(bf16[75,128]{0,1:T(8,128)(2,1)S(1)} %collective-permute-done.33), channel_id=1, source_target_pairs={{0,8},{1,9},{2,10},{3,11},{4,12},{5,13},{6,14},{7,15},{8,0},{9,1},... | collective-permute-start | bytes 57608 | tf_op jit(solution)/shard_map/ppermute | solution.py:9
  155.0 8.3 %collective-permute-start.17 = (bf16[48,10,1]{2,0,1:T(8,128)(2,1)S(1)}, bf16[48,10,1]{2,0,1:T(8,128)(2,1)S(1)}, u32[]{:S(2)}, u32[]{:S(2)}) collective-permute-start(bf16[48,10,1]{2,0,1:T(8,128)(2,1)S(1)} %get-tuple-element.142), channel_id=1, source_target_pairs={{1,0},{2,1},{3,2},{4,3},{5,4},{6,5},{7,6},{8,7},{9,8},{10,9},{11,1... | collective-permute-start | bytes 2888 | tf_op jit(solution)/shard_map/ppermute | solution.py:20
  159.4 5.1 %collective-permute-start.16 = (bf16[48,10,1]{2,0,1:T(8,128)(2,1)S(1)}, bf16[48,10,1]{2,0,1:T(8,128)(2,1)S(1)}, u32[]{:S(2)}, u32[]{:S(2)}) collective-permute-start(bf16[48,10,1]{2,0,1:T(8,128)(2,1)S(1)} %get-tuple-element.143), channel_id=1, source_target_pairs={{0,1},{1,2},{2,3},{3,4},{4,5},{5,6},{6,7},{7,8},{8,9},{9,10},{10,1... | collective-permute-start | bytes 2888 | tf_op jit(solution)/shard_map/ppermute | solution.py:19
  167.4 6.2 %collective-permute-start.35 = (bf16[75,128]{0,1:T(8,128)(2,1)S(1)}, bf16[75,128]{0,1:T(8,128)(2,1)S(1)}, u32[]{:S(2)}, u32[]{:S(2)}) collective-permute-start(bf16[75,128]{0,1:T(8,128)(2,1)S(1)} %collective-permute-done.34), channel_id=1, source_target_pairs={{0,16},{1,17},{2,18},{3,19},{4,20},{5,21},{6,22},{7,23},{8,24},{9,... | collective-permute-start | bytes 57608 | tf_op jit(solution)/shard_map/ppermute | solution.py:9
  171.7 0.7 copy-start.4
  445.5 1.7 copy-start.5
Sparse Core Ops, SparseCore 0:
  172.6 272.8 all-reduce.4
where the time goes:
time: 456 us; the launch traced here: 455 us
  waiting for transfers between devices  283 us (62%)
  starting transfers between devices  133 us (29%)
  between operations  15.3 us (3%)
  matrix products  13.4 us (3%)
  local copies, waits for them, and re-layouts  5.33 us (1%)
  other arithmetic  4.94 us (1%)
    psum x1, waiting for transfers between devices, body(): grad_w1, grad_w2 = lax.psum((term_w1, term_w2), ('lat', 'lon'))  271 us
    ppermute x20, starting transfers between devices, from_partner(): lax.ppermute(x, axis, [(i, i ^ 1 << bit) for i in range(lax.axis_size(axi...  79.5 us
    ppermute x8, starting transfers between devices, extended(): before = lax.ppermute(last, axis, up)  29.3 us
    ppermute x8, starting transfers between devices, extended(): after = lax.ppermute(leading, axis, down)  24.3 us
  transfers between devices with their start and end apart: 37, of which 11 were waited for; matrix products, arithmetic and copies ran while one was open for 3% of the time, Pallas kernels for 0%

commit v1 on v0

--- a/solution.py
+++ b/solution.py
@@ -139,7 +139,7 @@
     term_w1 = wgrad(grad_a, x_ext)
     grad_x_ext = tconv(grad_a, w1)
     dx = retract(grad_x_ext).astype(jnp.bfloat16)
-    grad_w1, grad_w2 = lax.psum((term_w1, term_w2), ("lat", "lon"))
+    grad_w1, grad_w2 = lax.psum(lax.psum((term_w1, term_w2), "lon"), "lat")
     cells = fields.shape[1] * fields.shape[2] * lax.axis_size("lat") * lax.axis_size("lon")
     factor = 1.0 / math.sqrt(cells)
     return (out_block, dx, grad_w1 * factor, grad_w2 * factor)

time: 456 us -> 587 us (1.29); the launches traced: 455 us -> 577 us
  waiting for transfers between devices: 283 us -> 404 us
    psum x1 -> x2, waiting for transfers between devices: 271 us -> 392 us  [body(): grad_w1, grad_w2 = lax.psum(lax.psum((term_w1, term_w2), 'lon'), 'lat')]
  transfers between devices with their start and end apart: 37 -> 38, of which waited for: 11 -> 12; matrix products, arithmetic and copies ran while one was open for 3% -> 2% of each run, Pallas kernels for 0% -> 0%
where the time goes in v1:
time: 587 us; the launch traced here: 577 us
  waiting for transfers between devices  404 us (69%)
  starting transfers between devices  133 us (23%)
  between operations  15.3 us (3%)
  matrix products  13.4 us (2%)
  local copies, waits for them, and re-layouts  5.97 us (1%)
    psum x2, waiting for transfers between devices, body(): grad_w1, grad_w2 = lax.psum(lax.psum((term_w1, term_w2), 'lon'), 'lat')  392 us
    ppermute x20, starting transfers between devices, from_partner(): lax.ppermute(x, axis, [(i, i ^ 1 << bit) for i in range(lax.axis_size(axi...  79.6 us
    ppermute x8, starting transfers between devices, extended(): before = lax.ppermute(last, axis, up)  29.3 us
    ppermute x8, starting transfers between devices, extended(): after = lax.ppermute(leading, axis, down)  24.3 us
  transfers between devices with their start and end apart: 38, of which 12 were waited for; matrix products, arithmetic and copies ran while one was open for 2% of the time, Pallas kernels for 0%

profile of v1, /device:TPU:1, one launch (start us, length us, event | category | flops | bytes accessed | tf_op | source)
XLA Modules:
  0.0 576.5 jit_solution(6585898775259117079)
XLA Ops:
  8.0 0.9 copy_multiply_fusion
  11.8 4.6 collective-permute-start.18
  16.4 6.1 %collective-permute-start.19 = (f32[1,48,10]{1,0,2:T(1,128)S(1)}, f32[1,48,10]{1,0,2:T(1,128)S(1)}, u32[]{:S(2)}, u32[]{:S(2)}) collective-permute-start(f32[1,48,10]{1,0,2:T(1,128)S(1)} %stack_squeeze.29), channel_id=1, source_target_pairs={{1,0},{2,1},{3,2},{4,3},{5,4},{6,5},{7,6},{8,7},{9,8},{10,9},{11,1... | collective-permute-start | bytes 5768 | tf_op jit(solution)/shard_map/ppermute | solution.py:20
  22.7 7.3 %collective-permute-start.1 = (bf16[75,128]{0,1:T(8,128)(2,1)S(1)}, bf16[75,128]{0,1:T(8,128)(2,1)S(1)}, u32[]{:S(2)}, u32[]{:S(2)}) collective-permute-start(bf16[75,128]{0,1:T(8,128)(2,1)S(1)} %bitcast.327), channel_id=1, source_target_pairs={{0,1},{1,0},{2,3},{3,2},{4,5},{5,4},{6,7},{7,6},{8,9},{9,8},{10,11... | collective-permute-start | bytes 57608 | tf_op jit(solution)/shard_map/ppermute | solution.py:9
  30.9 1.0 scatter-add.29
  31.9 1.9 collective-permute-start.2
  33.8 1.9 collective-permute-start.22
  35.8 1.1 collective-permute-done.22
  36.9 3.4 collective-permute-start.23
  40.3 1.9 collective-permute-start.3
  42.2 1.3 collective-permute-start.21
  43.5 4.3 collective-permute-start.24
  47.8 4.0 collective-permute-start.20
  51.8 1.9 collective-permute-start
  53.9 1.4 collective-permute-start.6
  55.4 2.8 collective-permute-start.25
  58.1 6.4 %collective-permute-start.4 = (bf16[75,128]{0,1:T(8,128)(2,1)S(1)}, bf16[75,128]{0,1:T(8,128)(2,1)S(1)}, u32[]{:S(2)}, u32[]{:S(2)}) collective-permute-start(bf16[75,128]{0,1:T(8,128)(2,1)S(1)} %collective-permute-done.3), channel_id=1, source_target_pairs={{0,8},{1,9},{2,10},{3,11},{4,12},{5,13},{6,14},{7,15},{8,0},{9,1},... | collective-permute-start | bytes 57608 | tf_op jit(solution)/shard_map/ppermute | solution.py:9
  64.7 2.0 collective-permute-start.26
  66.9 4.8 collective-permute-start.5
  72.0 1.1 collective-permute-done.5
  73.4 6.0 %collective-permute-start.8 = (bf16[75,10,1]{2,0,1:T(8,128)(2,1)S(1)}, bf16[75,10,1]{2,0,1:T(8,128)(2,1)S(1)}, u32[]{:S(2)}, u32[]{:S(2)}) collective-permute-start(bf16[75,10,1]{2,0,1:T(8,128)(2,1)S(1)} %get-tuple-element.136), channel_id=1, source_target_pairs={{1,0},{2,1},{3,2},{4,3},{5,4},{6,5},{7,6},{8,7},{9,8},{10,9},{11,1... | collective-permute-start | bytes 4508 | tf_op jit(solution)/shard_map/ppermute | solution.py:20
  79.5 3.1 collective-permute-start.7
  82.6 1.5 collective-permute-done.8
  84.1 1.2 collective-permute-done.7
  88.0 4.5 collective-permute-start.9
  92.5 7.7 %collective-permute-start.10 = (bf16[48,128]{1,0:T(8,128)(2,1)S(1)}, bf16[48,128]{1,0:T(8,128)(2,1)S(1)}, u32[]{:S(2)}, u32[]{:S(2)}) collective-permute-start(bf16[48,128]{1,0:T(8,128)(2,1)S(1)} %get-tuple-element.147), channel_id=1, source_target_pairs={{0,1},{1,0},{2,3},{3,2},{4,5},{5,4},{6,7},{7,6},{8,9},{9,8},{10,11... | collective-permute-start | bytes 36872 | tf_op jit(solution)/shard_map/ppermute | solution.py:9
  100.2 1.3 collective-permute-start.15
  106.6 1.9 collective-permute-start.27
  108.8 2.4 collective-permute-start.28
  111.3 2.7 collective-permute-done.28
  114.1 1.9 collective-permute-start.11
  116.1 5.3 collective-permute-start.31
  121.4 1.9 collective-permute-start.12
  124.2 1.3 collective-permute-start.30
  125.5 6.1 %collective-permute-start.29 = (bf16[1,75,128]{1,2,0:T(8,128)(2,1)S(1)}, bf16[1,75,128]{1,2,0:T(8,128)(2,1)S(1)}, u32[]{:S(2)}, u32[]{:S(2)}) collective-permute-start(bf16[1,75,128]{1,2,0:T(8,128)(2,1)S(1)} %get-tuple-element.130), channel_id=1, source_target_pairs={{0,32},{32,64},{64,96},{96,128},{128,160},{160,192},{192,224},{224... | collective-permute-start | bytes 57608 | tf_op jit(solution)/shard_map/ppermute | solution.py:19
  131.6 3.6 collective-permute-start.32
  135.3 8.4 %collective-permute-start.13 = (bf16[48,128]{1,0:T(8,128)(2,1)S(1)}, bf16[48,128]{1,0:T(8,128)(2,1)S(1)}, u32[]{:S(2)}, u32[]{:S(2)}) collective-permute-start(bf16[48,128]{1,0:T(8,128)(2,1)S(1)} %collective-permute-done.12), channel_id=1, source_target_pairs={{0,8},{1,9},{2,10},{3,11},{4,12},{5,13},{6,14},{7,15},{8,0},{9,1},... | collective-permute-start | bytes 36872 | tf_op jit(solution)/shard_map/ppermute | solution.py:9
  143.9 1.9 collective-permute-start.33
  145.8 2.7 collective-permute-start.14
  149.4 5.3 collective-permute-start.34
  155.0 4.4 collective-permute-start.17
  159.4 3.3 collective-permute-start.16
  163.3 1.2 collective-permute-done.16
  168.1 4.1 collective-permute-start.35
  173.2 1.1 collective-permute-done.35
  174.3 262.4 %all-reduce.7.cloned.1.call-done = (f32[9,48,75]{2,1,0:T(8,128)}, f32[9,48,48]{2,1,0:T(8,128)}) async-done(((f32[9,48,75]{2,1,0:T(8,128)}, f32[9,48,48]{2,1,0:T(8,128)}), (f32[9,48,75]{2,1,0:T(8,128)}, f32[9,48,48]{2,1,0:T(8,128)})) %all-reduce.7.cloned.1.call-update) | async-done | bytes 212560 | tf_op jit(solution)/shard_map/psum | solution.py:142
  437.7 129.6 %all-reduce.9.cloned.1.call-done = (f32[9,48,75]{2,1,0:T(8,128)}, f32[9,48,48]{2,1,0:T(8,128)}) async-done(((f32[9,48,75]{2,1,0:T(8,128)}, f32[9,48,48]{2,1,0:T(8,128)}), (f32[9,48,75]{2,1,0:T(8,128)}, f32[9,48,48]{2,1,0:T(8,128)})) %all-reduce.9.cloned.1.call-update) | async-done | bytes 212560 | tf_op jit(solution)/shard_map/psum | solution.py:142
  567.3 1.7 broadcast_multiply_fusion.1
  (146 shorter events, 22.5 us)
Async XLA Ops:
  7.2 1.7 copy-start.1
  7.2 429.5 %all-reduce.7.cloned.1.call-start = ((), (), s32[]{:S(2)}) async-start(), calls=%async_computation | async-start | bytes 884736 | tf_op jit(solution)/shard_map/psum | solution.py:142
  11.5 11.0 %copy-start = (bf16[75,8,128]{2,1,0:T(8,128)(2,1)S(1)}, bf16[75,8,128]{2,1,0:T(8,128)(2,1)}, u32[]{:S(2)}) copy-start(bf16[75,8,128]{2,1,0:T(8,128)(2,1)} %param.21) | copy-start | bytes 460804
  11.8 18.5 %collective-permute-start.18 = (f32[1,48,10]{1,0,2:T(1,128)S(1)}, f32[1,48,10]{1,0,2:T(1,128)S(1)}, u32[]{:S(2)}, u32[]{:S(2)}) collective-permute-start(f32[1,48,10]{1,0,2:T(1,128)S(1)} %stack_squeeze.28), channel_id=1, source_target_pairs={{0,1},{1,2},{2,3},{3,4},{4,5},{5,6},{6,7},{7,8},{8,9},{9,10},{10,1... | collective-permute-start | bytes 5768 | tf_op jit(solution)/shard_map/ppermute | solution.py:19
  16.4 13.7 %collective-permute-start.19 = (f32[1,48,10]{1,0,2:T(1,128)S(1)}, f32[1,48,10]{1,0,2:T(1,128)S(1)}, u32[]{:S(2)}, u32[]{:S(2)}) collective-permute-start(f32[1,48,10]{1,0,2:T(1,128)S(1)} %stack_squeeze.29), channel_id=1, source_target_pairs={{1,0},{2,1},{3,2},{4,3},{5,4},{6,5},{7,6},{8,7},{9,8},{10,9},{11,1... | collective-permute-start | bytes 5768 | tf_op jit(solution)/shard_map/ppermute | solution.py:20
  22.7 9.2 %collective-permute-start.1 = (bf16[75,128]{0,1:T(8,128)(2,1)S(1)}, bf16[75,128]{0,1:T(8,128)(2,1)S(1)}, u32[]{:S(2)}, u32[]{:S(2)}) collective-permute-start(bf16[75,128]{0,1:T(8,128)(2,1)S(1)} %bitcast.327), channel_id=1, source_target_pairs={{0,1},{1,0},{2,3},{3,2},{4,5},{5,4},{6,7},{7,6},{8,9},{9,8},{10,11... | collective-permute-start | bytes 57608 | tf_op jit(solution)/shard_map/ppermute | solution.py:9
  31.9 8.4 %collective-permute-start.2 = (bf16[75,128]{0,1:T(8,128)(2,1)S(1)}, bf16[75,128]{0,1:T(8,128)(2,1)S(1)}, u32[]{:S(2)}, u32[]{:S(2)}) collective-permute-start(bf16[75,128]{0,1:T(8,128)(2,1)S(1)} %collective-permute-done.1), channel_id=1, source_target_pairs={{0,2},{1,3},{2,0},{3,1},{4,6},{5,7},{6,4},{7,5},{8,10},{9,11},{10,... | collective-permute-start | bytes 57608 | tf_op jit(solution)/shard_map/ppermute | solution.py:9
  33.8 3.1 collective-permute-start.22
  36.9 6.6 %collective-permute-start.23 = (bf16[48,128]{1,0:T(8,128)(2,1)S(1)}, bf16[48,128]{1,0:T(8,128)(2,1)S(1)}, u32[]{:S(2)}, u32[]{:S(2)}) collective-permute-start(bf16[48,128]{1,0:T(8,128)(2,1)S(1)} %collective-permute-done.22), channel_id=1, source_target_pairs={{0,2},{1,3},{2,0},{3,1},{4,6},{5,7},{6,4},{7,5},{8,10},{9,11},{10,... | collective-permute-start | bytes 36872 | tf_op jit(solution)/shard_map/ppermute | solution.py:9
  40.3 17.9 %collective-permute-start.3 = (bf16[75,128]{0,1:T(8,128)(2,1)S(1)}, bf16[75,128]{0,1:T(8,128)(2,1)S(1)}, u32[]{:S(2)}, u32[]{:S(2)}) collective-permute-start(bf16[75,128]{0,1:T(8,128)(2,1)S(1)} %collective-permute-done.2), channel_id=1, source_target_pairs={{0,4},{1,5},{2,6},{3,7},{4,0},{5,1},{6,2},{7,3},{8,12},{9,13},{10,... | collective-permute-start | bytes 57608 | tf_op jit(solution)/shard_map/ppermute | solution.py:9
  42.2 11.7 %collective-permute-start.21 = (bf16[1,48,128]{2,1,0:T(8,128)(2,1)S(1)}, bf16[1,48,128]{2,1,0:T(8,128)(2,1)S(1)}, u32[]{:S(2)}, u32[]{:S(2)}) collective-permute-start(bf16[1,48,128]{2,1,0:T(8,128)(2,1)S(1)} %get-tuple-element.132), channel_id=1, source_target_pairs={{32,0},{64,32},{96,64},{128,96},{160,128},{192,160},{224,192},{256... | collective-permute-start | bytes 36872 | tf_op jit(solution)/shard_map/ppermute | solution.py:20
  43.5 11.8 %collective-permute-start.24 = (bf16[48,128]{1,0:T(8,128)(2,1)S(1)}, bf16[48,128]{1,0:T(8,128)(2,1)S(1)}, u32[]{:S(2)}, u32[]{:S(2)}) collective-permute-start(bf16[48,128]{1,0:T(8,128)(2,1)S(1)} %collective-permute-done.23), channel_id=1, source_target_pairs={{0,4},{1,5},{2,6},{3,7},{4,0},{5,1},{6,2},{7,3},{8,12},{9,13},{10,... | collective-permute-start | bytes 36872 | tf_op jit(solution)/shard_map/ppermute | solution.py:9
  47.8 16.8 %collective-permute-start.20 = (bf16[1,48,128]{2,1,0:T(8,128)(2,1)S(1)}, bf16[1,48,128]{2,1,0:T(8,128)(2,1)S(1)}, u32[]{:S(2)}, u32[]{:S(2)}) collective-permute-start(bf16[1,48,128]{2,1,0:T(8,128)(2,1)S(1)} %get-tuple-element.133), channel_id=1, source_target_pairs={{0,32},{32,64},{64,96},{96,128},{128,160},{160,192},{192,224},{224... | collective-permute-start | bytes 36872 | tf_op jit(solution)/shard_map/ppermute | solution.py:19
  51.8 12.8 %collective-permute-start = (bf16[75,1,128]{0,2,1:T(8,128)(2,1)S(1)}, bf16[75,1,128]{0,2,1:T(8,128)(2,1)S(1)}, u32[]{:S(2)}, u32[]{:S(2)}) collective-permute-start(bf16[75,1,128]{0,2,1:T(8,128)(2,1)S(1)} %copy.200), channel_id=1, source_target_pairs={{0,32},{32,64},{64,96},{96,128},{128,160},{160,192},{192,224},{224... | collective-permute-start | bytes 57608 | tf_op jit(solution)/shard_map/ppermute | solution.py:19
  53.9 17.8 %copy-start.2 = (bf16[9,48,75]{2,1,0:T(8,128)(2,1)S(1)}, bf16[9,48,75]{2,1,0:T(8,128)(2,1)}, u32[]{:S(2)}) copy-start(bf16[9,48,75]{2,1,0:T(8,128)(2,1)} %param.23) | copy-start | bytes 194404
  53.9 19.2 %collective-permute-start.6 = (bf16[75,1,128]{0,2,1:T(8,128)(2,1)S(1)}, bf16[75,1,128]{0,2,1:T(8,128)(2,1)S(1)}, u32[]{:S(2)}, u32[]{:S(2)}) collective-permute-start(bf16[75,1,128]{0,2,1:T(8,128)(2,1)S(1)} %copy.201), channel_id=1, source_target_pairs={{32,0},{64,32},{96,64},{128,96},{160,128},{192,160},{224,192},{256... | collective-permute-start | bytes 57608 | tf_op jit(solution)/shard_map/ppermute | solution.py:20
  55.4 9.4 %collective-permute-start.25 = (bf16[48,128]{1,0:T(8,128)(2,1)S(1)}, bf16[48,128]{1,0:T(8,128)(2,1)S(1)}, u32[]{:S(2)}, u32[]{:S(2)}) collective-permute-start(bf16[48,128]{1,0:T(8,128)(2,1)S(1)} %collective-permute-done.24), channel_id=1, source_target_pairs={{0,8},{1,9},{2,10},{3,11},{4,12},{5,13},{6,14},{7,15},{8,0},{9,1},... | collective-permute-start | bytes 36872 | tf_op jit(solution)/shard_map/ppermute | solution.py:9
  58.1 8.8 %collective-permute-start.4 = (bf16[75,128]{0,1:T(8,128)(2,1)S(1)}, bf16[75,128]{0,1:T(8,128)(2,1)S(1)}, u32[]{:S(2)}, u32[]{:S(2)}) collective-permute-start(bf16[75,128]{0,1:T(8,128)(2,1)S(1)} %collective-permute-done.3), channel_id=1, source_target_pairs={{0,8},{1,9},{2,10},{3,11},{4,12},{5,13},{6,14},{7,15},{8,0},{9,1},... | collective-permute-start | bytes 57608 | tf_op jit(solution)/shard_map/ppermute | solution.py:9
  64.7 7.2 %collective-permute-start.26 = (bf16[48,128]{1,0:T(8,128)(2,1)S(1)}, bf16[48,128]{1,0:T(8,128)(2,1)S(1)}, u32[]{:S(2)}, u32[]{:S(2)}) collective-permute-start(bf16[48,128]{1,0:T(8,128)(2,1)S(1)} %collective-permute-done.25), channel_id=1, source_target_pairs={{0,16},{1,17},{2,18},{3,19},{4,20},{5,21},{6,22},{7,23},{8,24},{9,... | collective-permute-start | bytes 36872 | tf_op jit(solution)/shard_map/ppermute | solution.py:9
  66.9 6.2 %collective-permute-start.5 = (bf16[75,128]{0,1:T(8,128)(2,1)S(1)}, bf16[75,128]{0,1:T(8,128)(2,1)S(1)}, u32[]{:S(2)}, u32[]{:S(2)}) collective-permute-start(bf16[75,128]{0,1:T(8,128)(2,1)S(1)} %collective-permute-done.4), channel_id=1, source_target_pairs={{0,16},{1,17},{2,18},{3,19},{4,20},{5,21},{6,22},{7,23},{8,24},{9,... | collective-permute-start | bytes 57608 | tf_op jit(solution)/shard_map/ppermute | solution.py:9
  73.4 10.7 %collective-permute-start.8 = (bf16[75,10,1]{2,0,1:T(8,128)(2,1)S(1)}, bf16[75,10,1]{2,0,1:T(8,128)(2,1)S(1)}, u32[]{:S(2)}, u32[]{:S(2)}) collective-permute-start(bf16[75,10,1]{2,0,1:T(8,128)(2,1)S(1)} %get-tuple-element.136), channel_id=1, source_target_pairs={{1,0},{2,1},{3,2},{4,3},{5,4},{6,5},{7,6},{8,7},{9,8},{10,9},{11,1... | collective-permute-start | bytes 4508 | tf_op jit(solution)/shard_map/ppermute | solution.py:20
  79.5 5.8 %collective-permute-start.7 = (bf16[75,10,1]{2,0,1:T(8,128)(2,1)S(1)}, bf16[75,10,1]{2,0,1:T(8,128)(2,1)S(1)}, u32[]{:S(2)}, u32[]{:S(2)}) collective-permute-start(bf16[75,10,1]{2,0,1:T(8,128)(2,1)S(1)} %get-tuple-element.137), channel_id=1, source_target_pairs={{0,1},{1,2},{2,3},{3,4},{4,5},{5,6},{6,7},{7,8},{8,9},{9,10},{10,1... | collective-permute-start | bytes 4508 | tf_op jit(solution)/shard_map/ppermute | solution.py:19
  88.0 37.5 %collective-permute-start.9 = (bf16[48,1,128]{2,0,1:T(8,128)(2,1)S(1)}, bf16[48,1,128]{2,0,1:T(8,128)(2,1)S(1)}, u32[]{:S(2)}, u32[]{:S(2)}) collective-permute-start(bf16[48,1,128]{2,0,1:T(8,128)(2,1)S(1)} %get-tuple-element.146), channel_id=1, source_target_pairs={{0,32},{32,64},{64,96},{96,128},{128,160},{160,192},{192,224},{224... | collective-permute-start | bytes 36872 | tf_op jit(solution)/shard_map/ppermute | solution.py:19
  92.5 21.6 %collective-permute-start.10 = (bf16[48,128]{1,0:T(8,128)(2,1)S(1)}, bf16[48,128]{1,0:T(8,128)(2,1)S(1)}, u32[]{:S(2)}, u32[]{:S(2)}) collective-permute-start(bf16[48,128]{1,0:T(8,128)(2,1)S(1)} %get-tuple-element.147), channel_id=1, source_target_pairs={{0,1},{1,0},{2,3},{3,2},{4,5},{5,4},{6,7},{7,6},{8,9},{9,8},{10,11... | collective-permute-start | bytes 36872 | tf_op jit(solution)/shard_map/ppermute | solution.py:9
  100.2 54.6 %collective-permute-start.15 = (bf16[48,1,128]{2,0,1:T(8,128)(2,1)S(1)}, bf16[48,1,128]{2,0,1:T(8,128)(2,1)S(1)}, u32[]{:S(2)}, u32[]{:S(2)}) collective-permute-start(bf16[48,1,128]{2,0,1:T(8,128)(2,1)S(1)} %get-tuple-element.148), channel_id=1, source_target_pairs={{32,0},{64,32},{96,64},{128,96},{160,128},{192,160},{224,192},{256... | collective-permute-start | bytes 36872 | tf_op jit(solution)/shard_map/ppermute | solution.py:20
  106.6 4.6 collective-permute-start.27
  108.8 5.2 collective-permute-start.28
  114.1 7.2 %collective-permute-start.11 = (bf16[48,128]{1,0:T(8,128)(2,1)S(1)}, bf16[48,128]{1,0:T(8,128)(2,1)S(1)}, u32[]{:S(2)}, u32[]{:S(2)}) collective-permute-start(bf16[48,128]{1,0:T(8,128)(2,1)S(1)} %collective-permute-done.10), channel_id=1, source_target_pairs={{0,2},{1,3},{2,0},{3,1},{4,6},{5,7},{6,4},{7,5},{8,10},{9,11},{10,... | collective-permute-start | bytes 36872 | tf_op jit(solution)/shard_map/ppermute | solution.py:9
  116.1 15.5 %collective-permute-start.31 = (bf16[75,128]{0,1:T(8,128)(2,1)S(1)}, bf16[75,128]{0,1:T(8,128)(2,1)S(1)}, u32[]{:S(2)}, u32[]{:S(2)}) collective-permute-start(bf16[75,128]{0,1:T(8,128)(2,1)S(1)} %get-tuple-element.128), channel_id=1, source_target_pairs={{0,1},{1,0},{2,3},{3,2},{4,5},{5,4},{6,7},{7,6},{8,9},{9,8},{10,11... | collective-permute-start | bytes 57608 | tf_op jit(solution)/shard_map/ppermute | solution.py:9
  121.4 13.9 %collective-permute-start.12 = (bf16[48,128]{1,0:T(8,128)(2,1)S(1)}, bf16[48,128]{1,0:T(8,128)(2,1)S(1)}, u32[]{:S(2)}, u32[]{:S(2)}) collective-permute-start(bf16[48,128]{1,0:T(8,128)(2,1)S(1)} %collective-permute-done.11), channel_id=1, source_target_pairs={{0,4},{1,5},{2,6},{3,7},{4,0},{5,1},{6,2},{7,3},{8,12},{9,13},{10,... | collective-permute-start | bytes 36872 | tf_op jit(solution)/shard_map/ppermute | solution.py:9
  123.5 0.7 copy-start.3
  124.2 24.2 %collective-permute-start.30 = (bf16[1,75,128]{1,2,0:T(8,128)(2,1)S(1)}, bf16[1,75,128]{1,2,0:T(8,128)(2,1)S(1)}, u32[]{:S(2)}, u32[]{:S(2)}) collective-permute-start(bf16[1,75,128]{1,2,0:T(8,128)(2,1)S(1)} %get-tuple-element.129), channel_id=1, source_target_pairs={{32,0},{64,32},{96,64},{128,96},{160,128},{192,160},{224,192},{256... | collective-permute-start | bytes 57608 | tf_op jit(solution)/shard_map/ppermute | solution.py:20
  125.5 22.9 %collective-permute-start.29 = (bf16[1,75,128]{1,2,0:T(8,128)(2,1)S(1)}, bf16[1,75,128]{1,2,0:T(8,128)(2,1)S(1)}, u32[]{:S(2)}, u32[]{:S(2)}) collective-permute-start(bf16[1,75,128]{1,2,0:T(8,128)(2,1)S(1)} %get-tuple-element.130), channel_id=1, source_target_pairs={{0,32},{32,64},{64,96},{96,128},{128,160},{160,192},{192,224},{224... | collective-permute-start | bytes 57608 | tf_op jit(solution)/shard_map/ppermute | solution.py:19
  131.6 12.2 %collective-permute-start.32 = (bf16[75,128]{0,1:T(8,128)(2,1)S(1)}, bf16[75,128]{0,1:T(8,128)(2,1)S(1)}, u32[]{:S(2)}, u32[]{:S(2)}) collective-permute-start(bf16[75,128]{0,1:T(8,128)(2,1)S(1)} %collective-permute-done.31), channel_id=1, source_target_pairs={{0,2},{1,3},{2,0},{3,1},{4,6},{5,7},{6,4},{7,5},{8,10},{9,11},{10,... | collective-permute-start | bytes 57608 | tf_op jit(solution)/shard_map/ppermute | solution.py:9
  135.3 10.5 %collective-permute-start.13 = (bf16[48,128]{1,0:T(8,128)(2,1)S(1)}, bf16[48,128]{1,0:T(8,128)(2,1)S(1)}, u32[]{:S(2)}, u32[]{:S(2)}) collective-permute-start(bf16[48,128]{1,0:T(8,128)(2,1)S(1)} %collective-permute-done.12), channel_id=1, source_target_pairs={{0,8},{1,9},{2,10},{3,11},{4,12},{5,13},{6,14},{7,15},{8,0},{9,1},... | collective-permute-start | bytes 36872 | tf_op jit(solution)/shard_map/ppermute | solution.py:9
  143.9 5.6 collective-permute-start.33
  145.8 9.0 %collective-permute-start.14 = (bf16[48,128]{1,0:T(8,128)(2,1)S(1)}, bf16[48,128]{1,0:T(8,128)(2,1)S(1)}, u32[]{:S(2)}, u32[]{:S(2)}) collective-permute-start(bf16[48,128]{1,0:T(8,128)(2,1)S(1)} %collective-permute-done.13), channel_id=1, source_target_pairs={{0,16},{1,17},{2,18},{3,19},{4,20},{5,21},{6,22},{7,23},{8,24},{9,... | collective-permute-start | bytes 36872 | tf_op jit(solution)/shard_map/ppermute | solution.py:9
  149.4 18.7 %collective-permute-start.34 = (bf16[75,128]{0,1:T(8,128)(2,1)S(1)}, bf16[75,128]{0,1:T(8,128)(2,1)S(1)}, u32[]{:S(2)}, u32[]{:S(2)}) collective-permute-start(bf16[75,128]{0,1:T(8,128)(2,1)S(1)} %collective-permute-done.33), channel_id=1, source_target_pairs={{0,8},{1,9},{2,10},{3,11},{4,12},{5,13},{6,14},{7,15},{8,0},{9,1},... | collective-permute-start | bytes 57608 | tf_op jit(solution)/shard_map/ppermute | solution.py:9
  155.0 8.3 %collective-permute-start.17 = (bf16[48,10,1]{2,0,1:T(8,128)(2,1)S(1)}, bf16[48,10,1]{2,0,1:T(8,128)(2,1)S(1)}, u32[]{:S(2)}, u32[]{:S(2)}) collective-permute-start(bf16[48,10,1]{2,0,1:T(8,128)(2,1)S(1)} %get-tuple-element.144), channel_id=1, source_target_pairs={{1,0},{2,1},{3,2},{4,3},{5,4},{6,5},{7,6},{8,7},{9,8},{10,9},{11,1... | collective-permute-start | bytes 2888 | tf_op jit(solution)/shard_map/ppermute | solution.py:20
  159.4 5.1 collective-permute-start.16
  166.9 0.7 copy-start.4
  167.6 399.7 %all-reduce.9.cloned.1.call-start = ((), (), s32[]{:S(2)}) async-start(), calls=%async_computation.1 | async-start | bytes 884736 | tf_op jit(solution)/shard_map/psum | solution.py:142
  168.1 6.2 %collective-permute-start.35 = (bf16[75,128]{0,1:T(8,128)(2,1)S(1)}, bf16[75,128]{0,1:T(8,128)(2,1)S(1)}, u32[]{:S(2)}, u32[]{:S(2)}) collective-permute-start(bf16[75,128]{0,1:T(8,128)(2,1)S(1)} %collective-permute-done.34), channel_id=1, source_target_pairs={{0,16},{1,17},{2,18},{3,19},{4,20},{5,21},{6,22},{7,23},{8,24},{9,... | collective-permute-start | bytes 57608 | tf_op jit(solution)/shard_map/ppermute | solution.py:9
  567.3 1.7 copy-start.5
Sparse Core Ops, SparseCore 0:
  167.8 268.9 all-reduce.6
  440.0 127.2 all-reduce.8
